TPU v7x, 128 devices: a whole 4x4x4 slice. The times are simulated.
128 devices in a mesh: pts: 32 (over z, y, core), grp: 4 (over x).
Axes of the slice: x: 4, y: 4, z: 4, core: 2. Of those that a mesh axis runs over, the one named last changes fastest.
Arguments:
- nodes: bfloat16 [2, 131072, 256], P(None, ('pts', 'grp')), may hold values from -6 to 6
- cotangent: bfloat16 [2, 131072, 256], P(None, ('pts', 'grp')), may hold values from -6 to 6
- first_inward: bfloat16 [256, 768], replicated, may hold values from -0.375 to 0.375
- first_outward: bfloat16 [256, 256], replicated, may hold values from -0.375 to 0.375
- second_inward: bfloat16 [256, 768], replicated, may hold values from -0.375 to 0.375
- second_outward: bfloat16 [256, 256], replicated, may hold values from -0.375 to 0.375
- rotated_source: int32 [2, 131072], P(None, ('pts', 'grp')), may hold values from 0 to 131071, as said below
- rotated_index: int32 [2, 131072], P(None, ('pts', 'grp')), may hold values from 0 to 131071, as said below
Outputs:
- input_grad: bfloat16 [2, 131072, 256], P(None, ('pts', 'grp'))
- first_inward_grad: float32 [256, 768], replicated
- first_outward_grad: float32 [256, 256], replicated
- second_inward_grad: float32 [256, 768], replicated
- second_outward_grad: float32 [256, 256], replicated
Inputs may be any that keep to these rules, and one draw needn't show every extreme that they name: For each sample, rotated_source and rotated_index are inverse permutations of the 131072 node indices. Split the indices into 128 aligned runs of 1024, one a device in the order of pts+grp. A node of run s has its rotated position in run t only where t - s, taken modulo 128, lies within -8 to 8. For every pair of different runs, at most 32 nodes of the first have their rotated position in the second, and exactly 32 for some pair. `rotated_index`: the inverse of rotated_source, sample by sample.
All inputs are finite; a program needn't handle non-finite values.
Results may differ from a plain program's by a relative error of at most 0.014.
Values may be sent and summed in bfloat16 or wider, within the bound.
No kernel may reach another device: no remote copies, remote signals or barrier semaphores. Data moves between devices by JAX's collectives and lax.ppermute only.
A program may use at most 128 MiB of HBM per device.

v0:
```python
import functools
import math

import jax
import jax.numpy as jnp
from jax import lax
from jax.experimental import pallas as pl
from jax.experimental.pallas import tpu as pltpu
from jax.sharding import PartitionSpec as P

HEADS = 8
BALL = 256
SPAN = 8
CAP = 32
EPSILON = 1e-06
AXES = ("pts", "grp")
GROUP = 4
HOPS = tuple(range(-(SPAN // GROUP), SPAN // GROUP + 1))
REACH = len(HOPS)
SLOTS = REACH * GROUP * CAP
LANDED = REACH + GROUP - 1
VMEM_LIMIT = 28 * 1024 * 1024

f32 = jnp.float32
bf16 = jnp.bfloat16


def dot(left, right, left_dim=1, right_dim=0):
    return lax.dot_general(
        left, right, (((left_dim,), (right_dim,)), ((), ())), preferred_element_type=f32
    )


def spread_column(row):
    return jnp.transpose(jnp.broadcast_to(row.astype(f32), (128, row.shape[1])))


def one_hot_rows(slot_row, slots):
    ids = lax.broadcasted_iota(jnp.int32, (slots, slot_row.shape[1]), 0)
    return jnp.where(ids == slot_row, 1.0, 0.0).astype(bf16)


def one_hot_picks(pick_column, start, width):
    lanes = lax.broadcasted_iota(jnp.int32, pick_column.shape, 1).astype(f32)
    pieces = [
        jnp.where(pick_column == lanes + float(start + 128 * piece), 1.0, 0.0).astype(bf16)
        for piece in range(width // 128)
    ]
    return jnp.concatenate(pieces, axis=1)


def same_before(column, row, row_ids, lane_ids):
    counts = []
    for piece in range(row.shape[1] // 128):
        lanes = slice(128 * piece, 128 * piece + 128)
        same = (column == row[:, lanes]) & (row_ids < lane_ids + float(128 * piece))
        counts.append(jnp.sum(jnp.where(same, 1.0, 0.0), axis=0, keepdims=True))
    return jnp.concatenate(counts, axis=1).astype(jnp.int32)


def count_between(column, floor_row, row):
    counts = []
    for piece in range(row.shape[1] // 128):
        lanes = slice(128 * piece, 128 * piece + 128)
        inside = (column >= floor_row[:, lanes]) & (column < row[:, lanes])
        counts.append(jnp.sum(jnp.where(inside, 1.0, 0.0), axis=0, keepdims=True))
    return jnp.concatenate(counts, axis=1).astype(jnp.int32)


def slots_of(shard, own, rank, shards):
    member = (shard - own) & (GROUP - 1)
    hop = ((shard // GROUP) - (own // GROUP) + REACH // 2) & (shards // GROUP - 1)
    leave = (hop * GROUP + member) * CAP + rank
    land = (((-member) & (GROUP - 1)) * REACH + (REACH - 1 - hop)) * CAP + rank
    return leave, land


def send_kernel(own_ref, index_ref, meta_ref, *, shards):
    samples, rows = index_ref.shape
    own = own_ref[0]
    row_ids = lax.broadcasted_iota(jnp.int32, (rows, 128), 0).astype(f32)
    lane_ids = lax.broadcasted_iota(jnp.int32, (rows, 128), 1).astype(f32)
    for sample in range(samples):
        index = index_ref[sample : sample + 1, :]
        shard = index // rows
        rank = same_before(spread_column(shard), shard.astype(f32), row_ids, lane_ids)
        leave, land = slots_of(shard, own, rank, shards)
        meta_ref[sample : sample + 1, :] = jnp.where(shard == own, -1, leave)
        meta_ref[samples + sample : samples + sample + 1, :] = jnp.where(
            shard == own, index - own * rows, rows + land
        )


def receive_kernel(own_ref, source_ref, meta_ref, *, shards):
    samples, rows = source_ref.shape
    own = own_ref[0]
    for sample in range(samples):
        source = source_ref[sample : sample + 1, :]
        shard = source // rows
        floor_row = (shard * rows).astype(f32)
        rank = count_between(spread_column(source), floor_row, source.astype(f32))
        leave, land = slots_of(shard, own, rank, shards)
        meta_ref[sample : sample + 1, :] = jnp.where(shard == own, -1, leave)
        meta_ref[samples + sample : samples + sample + 1, :] = jnp.where(
            shard == own, source - own * rows, rows + land
        )


LOG2E = 1.4426950408889634
JOINED = 4


def masked(array, mask):
    return jnp.where(mask, array, jnp.zeros_like(array))


def head_masks(width):
    heads = lax.broadcasted_iota(jnp.int32, (BALL, width), 1) // (width // HEADS)
    own = [heads == head for head in range(HEADS)]
    return own, own[1:] + own[:1]


def norm(rows):
    widened = rows.astype(f32)
    row_scale = lax.rsqrt(jnp.mean(widened * widened, axis=-1, keepdims=True) + EPSILON)
    return widened, row_scale, (widened * row_scale).astype(bf16)


def score_factor(width):
    return LOG2E * (width // HEADS) ** (-0.5)


def project(normed, inward):
    width = normed.shape[1]
    mixture = dot(normed, inward)
    query_raw = mixture[:, :width]
    key_raw = mixture[:, width : 2 * width]
    query_scale = lax.rsqrt(jnp.mean(query_raw * query_raw, axis=-1, keepdims=True) + EPSILON)
    key_scale = lax.rsqrt(jnp.mean(key_raw * key_raw, axis=-1, keepdims=True) + EPSILON)
    query_unit = query_raw * query_scale
    key_unit = key_raw * key_scale
    rounded = (
        (query_unit * score_factor(width)).astype(bf16),
        key_unit.astype(bf16),
        mixture[:, 2 * width :].astype(bf16),
    )
    return (query_unit, query_scale, key_unit, key_scale), rounded


def key_weights(own_keys, queries):
    return jnp.exp2(dot(own_keys, queries, 1, 1))


def attend(queries, key_rows, values):
    width = queries.shape[1]
    half = width // 2
    own, _ = head_masks(width)
    results = []
    for start in range(0, HEADS, HEADS // 2):
        weights = []
        rights = []
        for head in range(start, start + HEADS // 2):
            scores = dot(masked(queries, own[head]), key_rows, 1, 1)
            weights.append(jnp.exp2(scores).astype(bf16))
            opposite = own[(head + HEADS // 2) % HEADS]
            ones = jnp.where(opposite, jnp.ones_like(values), jnp.zeros_like(values))
            rights.append(jnp.where(own[head], values, ones))
        results.append(dot(jnp.concatenate(weights, axis=1), jnp.concatenate(rights, axis=0)))
    low, high = results
    sums = jnp.concatenate([low[:, :half], high[:, half:]], axis=1)
    inverse = 1.0 / jnp.concatenate([low[:, half:], high[:, :half]], axis=1)
    return sums * inverse, inverse


def attend_backward(
    queries, key_rows, values, attended, inverse, grad_attended, kept_weights=None
):
    width = queries.shape[1]
    depth = width // HEADS
    own, after = head_masks(width)
    scaled = (grad_attended * inverse).astype(bf16)
    product = scaled.astype(f32) * attended
    high = product.astype(bf16)
    low = (product - high.astype(f32)).astype(bf16)
    groups = lax.broadcasted_iota(jnp.int32, (width, width), 0) // depth
    same_head = groups == lax.broadcasted_iota(jnp.int32, (width, width), 1) // depth
    group_ones = jnp.where(same_head, 1.0, 0.0).astype(bf16)
    column_sum = pltpu.roll(dot(high, group_ones) + dot(low, group_ones), depth, 1)
    column_high = column_sum.astype(bf16)
    column_low = (column_sum - column_high.astype(f32)).astype(bf16)
    lane = lax.broadcasted_iota(jnp.int32, (BALL, width), 1) % depth
    carried = jnp.where(lane == 0, column_high, masked(column_low, lane == 1))
    grad_queries = jnp.zeros((BALL, width), f32)
    grad_keys = jnp.zeros((BALL, width), f32)
    grad_values = jnp.zeros((BALL, width), f32)
    for start in range(0, HEADS, JOINED):
        weight_parts, score_parts, scaled_parts, query_parts, key_parts = [], [], [], [], []
        for head in range(start, start + JOINED):
            own_keys = masked(key_rows, own[head])
            left = jnp.where(own[head], scaled, masked(carried, after[head]))
            right = jnp.where(after[head], -jnp.ones_like(values), values)
            if kept_weights is None:
                weights = key_weights(own_keys, queries)
            else:
                weights = kept_weights[head * BALL : (head + 1) * BALL, :].astype(f32)
            score_parts.append((weights * dot(right, left, 1, 1)).astype(bf16))
            weight_parts.append(weights.astype(bf16))
            scaled_parts.append(masked(scaled, own[head]))
            query_parts.append(masked(queries, own[head]))
            key_parts.append(own_keys)
        grad_values += dot(
            jnp.concatenate(weight_parts, axis=1), jnp.concatenate(scaled_parts, axis=0)
        )
        grad_keys += dot(
            jnp.concatenate(score_parts, axis=1), jnp.concatenate(query_parts, axis=0)
        )
        grad_queries += dot(
            jnp.concatenate(score_parts, axis=0), jnp.concatenate(key_parts, axis=0), 0, 0
        )
    return grad_queries, grad_keys * (1.0 / LOG2E), grad_values


def ball_slices(rows):
    return [slice(start, start + BALL) for start in range(0, rows, BALL)]


def block_backward(
    kept, rounded, attended, inverse, grad_rows, inward, outward, weights_ref=None
):
    widened, row_scale, normed, query_unit, query_scale, key_unit, key_scale = kept
    width = widened.shape[1]
    grad_attended = dot(grad_rows, outward, 1, 1)
    parts = []
    for place, ball in enumerate(ball_slices(widened.shape[0])):
        kept_weights = None
        if weights_ref is not None:
            kept_weights = weights_ref[0, place * HEADS * BALL : (place + 1) * HEADS * BALL, :]
        parts.append(
            attend_backward(
                *(array[ball] for array in rounded),
                attended[ball].astype(f32),
                inverse[ball],
                grad_attended[ball],
                kept_weights,
            )
        )
    grad_queries, grad_keys, grad_values = (jnp.concatenate(p, axis=0) for p in zip(*parts))
    grad_queries = grad_queries * (width // HEADS) ** (-0.5)
    grad_qraw = query_scale * (
        grad_queries - query_unit * jnp.mean(grad_queries * query_unit, axis=-1, keepdims=True)
    )
    grad_kraw = key_scale * (
        grad_keys - key_unit * jnp.mean(grad_keys * key_unit, axis=-1, keepdims=True)
    )
    grad_mixture = jnp.concatenate([grad_qraw, grad_kraw, grad_values], axis=1).astype(bf16)
    grad_outward = dot(attended.astype(bf16), grad_rows, 0, 0)
    grad_inward = dot(normed, grad_mixture, 0, 0)
    grad_normed = dot(grad_mixture, inward, 1, 1)
    unit_rows = widened * row_scale
    grad_input = grad_rows.astype(f32) + row_scale * (
        grad_normed - unit_rows * jnp.mean(grad_normed * unit_rows, axis=-1, keepdims=True)
    )
    return grad_input.astype(bf16), grad_inward, grad_outward


def pack(slot_row, rows):
    return dot(one_hot_rows(slot_row, SLOTS), rows).astype(bf16)


def put_packets(packed, packet_refs):
    kinds, width = packet_refs[0].shape[2], packet_refs[0].shape[4]
    for hop in range(REACH):
        for member in range(GROUP):
            start = (hop * GROUP + member) * CAP
            for kind in range(kinds):
                part = packed[start : start + CAP, kind * width : (kind + 1) * width]
                packet_refs[hop][member, 0, kind] = part


def flat(refs):
    parts = [(ref, 0) for ref in refs[:REACH]]
    parts += [(ref, hop) for ref in refs[REACH:] for hop in range(REACH)]
    kinds = refs[0].shape[2]
    return [jnp.concatenate([ref[hop, 0, k] for ref, hop in parts], axis=0) for k in range(kinds)]


def add_up(total_ref, term):
    first = pl.program_id(0) == 0

    @pl.when(first)
    def _():
        total_ref[...] = term

    @pl.when(jnp.logical_not(first))
    def _():
        total_ref[...] += term


def join_grads(total_ref, inward_grad, outward_grad):
    width = outward_grad.shape[0]
    for third in range(3):
        part = inward_grad[:, third * width : (third + 1) * width]
        total_ref[third * width : (third + 1) * width, :] = part.astype(bf16)
    total_ref[3 * width : 4 * width, :] = outward_grad.astype(bf16)


def add_grads(total_ref, sum_refs, grads, other_ref=None):
    for sum_ref, grad in zip(sum_refs, grads):
        add_up(sum_ref, grad)

    @pl.when(pl.program_id(0) == pl.num_programs(0) - 1)
    def _():
        join_grads(total_ref, *(ref[...] for ref in sum_refs))
        if other_ref is not None:
            total_ref[other_ref.shape[0] :, :] = other_ref[...]


def sample_row(meta_ref, kind):
    samples = meta_ref.shape[0] // 2
    return meta_ref[pl.ds(kind * samples + pl.program_id(0), 1), :]


def attend_balls(rounded):
    rows = rounded[0].shape[0]
    parts = [attend(*(array[ball] for array in rounded)) for ball in ball_slices(rows)]
    attended, inverse = (jnp.concatenate(part, axis=0) for part in zip(*parts))
    return attended, inverse


def forward_kernel(nodes_ref, cot_ref, inward_ref, outward_ref, meta_ref, *refs):
    after_ref, attended_ref, inverse_ref, rounded_ref, scales_ref, *packet_refs = refs
    width = nodes_ref.shape[2]
    widened, _, normed = norm(nodes_ref[0])
    (_, query_scale, _, key_scale), rounded = project(normed, inward_ref[...])
    attended, inverse = attend_balls(rounded)
    attended = attended.astype(bf16)
    attended_ref[0] = attended
    inverse_ref[0] = inverse
    for place, array in enumerate(rounded):
        rounded_ref[0, :, place * width : (place + 1) * width] = array
    lane = lax.broadcasted_iota(jnp.int32, scales_ref.shape[1:], 1)
    scales_ref[0] = jnp.where(lane == 0, query_scale, key_scale)
    result = (widened + dot(attended, outward_ref[...])).astype(bf16)
    after_ref[0] = result
    both = jnp.concatenate([result, cot_ref[0]], axis=1)
    put_packets(pack(sample_row(meta_ref, 0), both), packet_refs)


def each_ball(rows, body):
    @pl.loop(0, rows // BALL)
    def _(ball):
        body(ball, pl.ds(pl.multiple_of(ball * BALL, BALL), BALL))


def weights_kernel(rounded_ref, weights_ref):
    width = rounded_ref.shape[2] // 3
    own, _ = head_masks(width)

    def body(ball, here):
        queries = rounded_ref[0, here, :width]
        key_rows = rounded_ref[0, here, width : 2 * width]
        for head in range(HEADS):
            start = pl.multiple_of((ball * HEADS + head) * BALL, BALL)
            weights = key_weights(masked(key_rows, own[head]), queries)
            weights_ref[0, pl.ds(start, BALL), :] = weights.astype(bf16)

    each_ball(rounded_ref.shape[1], body)


def near_kernel(meta_ref, *refs):
    *home_refs, near_ref, picks_ref = refs
    picks_ref[...] = spread_column(sample_row(meta_ref, 1))
    rows, width = home_refs[0].shape[1:]

    def body(ball, here):
        hits = one_hot_picks(picks_ref[here, :], 0, rows)
        for kind, home_ref in enumerate(home_refs):
            near = dot(hits, home_ref[0]).astype(bf16)
            near_ref[0, here, kind * width : (kind + 1) * width] = near

    each_ball(rows, body)


def add_far(meta_ref, near_ref, landed_refs):
    hits = one_hot_picks(spread_column(sample_row(meta_ref, 1)), near_ref.shape[1], SLOTS)
    rows = []
    for kind, landed in enumerate(flat(landed_refs)):
        width = landed.shape[1]
        near = near_ref[0, :, kind * width : (kind + 1) * width]
        rows.append((near.astype(f32) + dot(hits, landed)).astype(bf16))
    return rows


def second_kernel(meta_ref, near_ref, inward_ref, outward_ref, *refs):
    arrived_refs, refs = refs[:LANDED], refs[LANDED:]
    grad_ref, total_ref, *packet_refs = refs[: 2 + REACH]
    *sum_refs, rotated_ref, rotated_cot_ref = refs[2 + REACH :]

    @pl.when(pl.program_id(0) >= 0)
    def _():
        rotated_ref[...], rotated_cot_ref[...] = add_far(meta_ref, near_ref, arrived_refs)

    kept = norm(rotated_ref[...])
    units, rounded = project(kept[2], inward_ref[...])
    attended, inverse = attend_balls(rounded)
    grad_input, *grads = block_backward(
        kept + units,
        rounded,
        attended,
        inverse,
        rotated_cot_ref[...],
        inward_ref[...],
        outward_ref[...],
    )
    grad_ref[0] = grad_input
    add_grads(total_ref, sum_refs, grads)
    put_packets(pack(sample_row(meta_ref, 0), grad_input), packet_refs)


def first_kernel(
    meta_ref,
    nodes_ref,
    near_ref,
    attended_ref,
    inverse_ref,
    rounded_ref,
    scales_ref,
    weights_ref,
    inward_ref,
    outward_ref,
    *refs,
):
    returned_refs, refs = refs[:LANDED], refs[LANDED:]
    other_ref, grad_ref, total_ref, *sum_refs = refs
    (grad_after,) = add_far(meta_ref, near_ref, returned_refs)
    width = nodes_ref.shape[2]
    rounded = [rounded_ref[0, :, place * width : (place + 1) * width] for place in range(3)]
    query_unit = rounded[0].astype(f32) * (1.0 / score_factor(width))
    key_unit = rounded[1].astype(f32)
    units = (query_unit, scales_ref[0, :, 0:1], key_unit, scales_ref[0, :, 1:2])
    grad_input, *grads = block_backward(
        norm(nodes_ref[0]) + units,
        rounded,
        attended_ref[0],
        inverse_ref[0],
        grad_after,
        inward_ref[...],
        outward_ref[...],
        weights_ref,
    )
    grad_ref[0] = grad_input
    add_grads(total_ref, sum_refs, grads, other_ref)


def split_kernel(whole_ref, *refs):
    width = refs[1].shape[0]
    for place, (inward_ref, outward_ref) in enumerate((refs[:2], refs[2:])):
        start = place * 4 * width
        for third in range(3):
            part = whole_ref[start + third * width : start + (third + 1) * width, :]
            inward_ref[:, third * width : (third + 1) * width] = part.astype(f32)
        outward_ref[...] = whole_ref[start + 3 * width : start + 4 * width, :].astype(f32)


def full_spec(shape):
    return pl.BlockSpec(shape, lambda i: (0,) * len(shape))


def call(kernel, name, micros, in_specs, operands, outs, out_specs=None, steps=1, **options):
    specs = [
        full_spec(operand.shape) if spec is None else spec
        for spec, operand in zip(in_specs or [None] * len(operands), operands)
    ]
    return pl.pallas_call(
        kernel,
        name=name,
        grid=(steps,),
        in_specs=specs,
        out_specs=out_specs or [full_spec(out.shape) for out in outs],
        out_shape=outs,
        compiler_params=pltpu.CompilerParams(vmem_limit_bytes=VMEM_LIMIT),
        cost_estimate=pl.CostEstimate(
            flops=int(micros * 1.15e9), bytes_accessed=2**20, transcendentals=0
        ),
        **options,
    )(*operands)


def rotate(value, axis, steps):
    count = lax.axis_size(axis)
    pairs = [(source, (source + steps) % count) for source in range(count)]
    return lax.ppermute(value, axis, pairs)


def hop_stage(packets):
    return [p if hop == 0 else rotate(p, "pts", hop) for hop, p in zip(HOPS, packets)]


def restack(moved):
    return [
        jnp.concatenate([packet[member : member + 1] for packet in moved], axis=0)
        for member in range(1, GROUP)
    ]


def member_stage(moved, stacked):
    return moved + [rotate(s, "grp", 1 + place) for place, s in enumerate(stacked)]


def exchange(packets):
    moved = hop_stage(packets)
    return member_stage(moved, restack(moved))


def reduce_all(terms, factor):
    count = lax.axis_size(AXES)
    pieces = terms.reshape(count, -1, terms.shape[1])
    mine = lax.all_to_all(pieces, AXES, 0, 0, tiled=True)
    total = (jnp.sum(mine.astype(f32), axis=0) * factor).astype(bf16)
    spread = jnp.broadcast_to(total[None], pieces.shape)
    return lax.all_to_all(spread, AXES, 0, 0, tiled=True).reshape(terms.shape)


def per_device(
    nodes,
    cotangent,
    first_inward,
    first_outward,
    second_inward,
    second_outward,
    rotated_source,
    rotated_index,
):
    samples, rows, width = nodes.shape
    shards = lax.axis_size(AXES)
    own = lax.axis_index(AXES).astype(jnp.int32).reshape(1)
    shape = jax.ShapeDtypeStruct
    smem = pl.BlockSpec(memory_space=pltpu.SMEM)
    rows_shape = shape(nodes.shape, bf16)
    meta_shape = shape((2 * samples, rows), jnp.int32)
    joined_shape = shape((4 * width, width), bf16)
    both_shape = shape((8 * width, width), bf16)
    sums = [pltpu.VMEM((width, 3 * width), f32), pltpu.VMEM((width, width), f32)]
    first_weights = (first_inward, first_outward)
    second_weights = (second_inward, second_outward)

    def by_sample(*dims):
        return pl.BlockSpec((1, *dims), lambda s: (s, *(0 for _ in dims)))

    def packets(kinds):
        return [shape((GROUP, samples, kinds, CAP, width), bf16)] * REACH

    def packets_by_sample(kinds):
        return [pl.BlockSpec((GROUP, 1, kinds, CAP, width), lambda s: (0, s, 0, 0, 0))] * REACH

    def landed_by_sample(kinds):
        one = pl.BlockSpec((1, 1, kinds, CAP, width), lambda s: (0, s, 0, 0, 0))
        hops = pl.BlockSpec((REACH, 1, kinds, CAP, width), lambda s: (0, s, 0, 0, 0))
        return [one] * REACH + [hops] * (GROUP - 1)

    rows_spec = by_sample(rows, width)
    (send_meta,) = call(
        functools.partial(send_kernel, shards=shards),
        "send_places",
        2,
        [smem, None],
        (own, rotated_index),
        [meta_shape],
    )
    after_first, attended, inverse, rounded, scales, *out_packets = call(
        forward_kernel,
        "forward",
        9,
        [rows_spec, rows_spec, None, None, None],
        (nodes, cotangent, *first_weights, send_meta),
        [
            rows_shape,
            rows_shape,
            shape(nodes.shape, f32),
            shape((samples, rows, 3 * width), bf16),
            shape((samples, rows, 128), f32),
        ]
        + packets(2),
        [rows_spec] * 3
        + [by_sample(rows, 3 * width), by_sample(rows, 128)]
        + packets_by_sample(2),
        samples,
    )
    arrived = exchange(out_packets)
    (receive_meta,) = call(
        functools.partial(receive_kernel, shards=shards),
        "receive_places",
        2,
        [smem, None],
        (own, rotated_source),
        [meta_shape],
    )
    (near,) = call(
        near_kernel,
        "near_out",
        3,
        [None, rows_spec, rows_spec],
        (receive_meta, after_first, cotangent),
        [shape((samples, rows, 2 * width), bf16)],
        [by_sample(rows, 2 * width)],
        samples,
        scratch_shapes=[pltpu.VMEM((rows, 128), f32)],
    )
    weights_spec = by_sample(rows * HEADS, BALL)
    (weights,) = call(
        weights_kernel,
        "weights",
        6,
        [by_sample(rows, 3 * width)],
        (rounded,),
        [shape((samples, rows * HEADS, BALL), bf16)],
        [weights_spec],
        samples,
    )
    rotated_grad, second_joined, *back_packets = call(
        second_kernel,
        "second",
        26,
        [None, by_sample(rows, 2 * width), None, None] + landed_by_sample(2),
        (receive_meta, near, *second_weights, *arrived),
        [rows_shape, joined_shape] + packets(1),
        [rows_spec, full_spec(joined_shape.shape)] + packets_by_sample(1),
        samples,
        scratch_shapes=sums + [pltpu.VMEM((rows, width), bf16)] * 2,
    )
    returned = exchange(back_packets)
    (grad_near,) = call(
        near_kernel,
        "near_back",
        2,
        [None, rows_spec],
        (send_meta, rotated_grad),
        [rows_shape],
        [rows_spec],
        samples,
        scratch_shapes=[pltpu.VMEM((rows, 128), f32)],
    )
    input_grad, joined = call(
        first_kernel,
        "first",
        16,
        [None]
        + [rows_spec] * 4
        + [by_sample(rows, 3 * width), by_sample(rows, 128), weights_spec, None, None]
        + landed_by_sample(1)
        + [None],
        (
            send_meta,
            nodes,
            grad_near,
            attended,
            inverse,
            rounded,
            scales,
            weights,
            *first_weights,
            *returned,
            second_joined,
        ),
        [rows_shape, both_shape],
        [rows_spec, full_spec(both_shape.shape)],
        samples,
        scratch_shapes=sums,
    )
    factor = 1.0 / math.sqrt(samples * rows * shards)
    grad_shapes = [shape((width, 3 * width), f32), shape((width, width), f32)]
    grads = call(split_kernel, "split", 2, None, (reduce_all(joined, factor),), grad_shapes * 2)
    return (input_grad, *grads)


def solution(mesh):
    in_specs = (
        P(None, AXES, None),
        P(None, AXES, None),
        P(),
        P(),
        P(),
        P(),
        P(None, AXES),
        P(None, AXES),
    )
    out_specs = (P(None, AXES, None), P(), P(), P(), P())
    return jax.shard_map(
        per_device, mesh=mesh, in_specs=in_specs, out_specs=out_specs, check_vma=False
    )
```

profile of v0, /device:TPU:1, one launch (start us, length us, event | category | flops | bytes accessed | tf_op | source)
XLA Modules:
  0.0 169.8 jit_solution(6778539098112813793)
XLA Ops:
  0.6 0.7 copy-done.6
  1.3 1.3 send_places.1.meta_ref
  2.6 0.2 copy-done.1
  2.9 0.1 copy-done.3
  3.0 0.0 copy-done.5
  3.0 8.1 %forward.1 = (bf16[2,1024,256]{2,1,0:T(8,128)(2,1)S(1)}, bf16[2,1024,256]{2,1,0:T(8,128)(2,1)S(1)}, f32[2,1024,256]{2,1,0:T(8,128)S(1)}, bf16[2,1024,768]{2,1,0:...) custom-call(bf16[2,1024,256]{2,1,0:T(8,128)(2,1)S(1)} %copy-done.1, ...), custom_call_target="tpu_custom_call" | custom-call | flops 10350000128 | bytes 1048576 | tf_op jit(solution)/shard_map/forward/pallas_call | solution.py:474
  11.1 7.1 %collective-permute-start = (bf16[4,2,2,32,256]{4,3,2,1,0:T(8,128)(2,1)S(1)}, bf16[4,2,2,32,256]{4,3,2,1,0:T(8,128)(2,1)S(1)}, u32[]{:S(2)}, u32[]{:S(2)}) collective-permute-start(bf16[4,2,2,32,256]{4,3,2,1,0:T(8,128)(2,1)S(1)} %get-tuple-element.29), channel_id=1, source_target_pairs={{0,120},{4,124},{8,0},{12,4},{16,8},{20,12},{24,16},{28,20},{32,24... | collective-permute-start | bytes 786440 | tf_op jit(solution)/shard_map/ppermute | solution.py:492
  18.2 1.0 collective-permute-start.1
  19.2 0.8 collective-permute-start.2
  20.0 0.0 collective-permute-start.3
  20.0 3.2 %collective-permute-done.refs_0_ = bf16[4,2,2,32,256]{4,3,2,1,0:T(8,128)(2,1)S(1)} collective-permute-done((bf16[4,2,2,32,256]{4,3,2,1,0:T(8,128)(2,1)S(1)}, bf16[4,2,2,32,256]{4,3,2,1,0:T(8,128)(2,1)S(1)}, u32[]{:S(2)}, u32[]{:S(2)}) %collective-permute-start) | collective-permute-done | bytes 262176 | tf_op jit(solution)/shard_map/ppermute | solution.py:492
  23.2 0.8 collective-permute-done.1.refs_1_
  24.1 1.5 collective-permute-done.2.refs_3_
  25.5 7.7 %collective-permute-done.3.refs_4_ = bf16[4,2,2,32,256]{4,3,2,1,0:T(8,128)(2,1)S(1)} collective-permute-done((bf16[4,2,2,32,256]{4,3,2,1,0:T(8,128)(2,1)S(1)}, bf16[4,2,2,32,256]{4,3,2,1,0:T(8,128)(2,1)S(1)}, u32[]{:S(2)}, u32[]{:S(2)}) %collective-permute-start.3) | collective-permute-done | bytes 262176 | tf_op jit(solution)/shard_map/ppermute | solution.py:492
  33.2 2.5 %collective-permute-start.6 = (bf16[5,2,2,32,256]{4,3,2,1,0:T(8,128)(2,1)S(1)}, bf16[5,2,2,32,256]{4,3,2,1,0:T(8,128)(2,1)S(1)}, u32[]{:S(2)}, u32[]{:S(2)}) collective-permute-start(bf16[5,2,2,32,256]{4,3,2,1,0:T(8,128)(2,1)S(1)} %get-tuple-element.51), channel_id=1, source_target_pairs={{0,3},{1,0},{2,1},{3,2},{4,7},{5,4},{6,5},{7,6},{8,11},{9,8},{10,9... | collective-permute-start | bytes 983048 | tf_op jit(solution)/shard_map/ppermute | solution.py:492
  35.8 0.5 collective-permute-start.5
  36.3 0.6 collective-permute-start.4
  36.9 1.5 receive_places.1.meta_ref
  38.4 0.0 copy-start.2
  38.4 0.0 copy-start.4
  38.4 4.0 %near_out.1.near_ref = bf16[2,1024,512]{2,1,0:T(8,128)(2,1)S(1)} custom-call(s32[4,1024]{1,0:T(4,128)S(1)} %receive_places.1.meta_ref, bf16[2,1024,256]{2,1,0:T(8,128)(2,1)S(1)} %get-tuple-element.28.refs_0_, bf16[2,1024,256]{2,1,0:T(8,128)(2,1)S(1)} %copy-done), custom_call_target="tpu_custom_call" | custom-call | flops 3449999872 | bytes 1048576 | tf_op jit(solution)/shard_map/near_out/pallas_call | solution.py:474
  42.4 7.4 %collective-permute-done.6.refs_7_ = bf16[5,2,2,32,256]{4,3,2,1,0:T(8,128)(2,1)S(1)} collective-permute-done((bf16[5,2,2,32,256]{4,3,2,1,0:T(8,128)(2,1)S(1)}, bf16[5,2,2,32,256]{4,3,2,1,0:T(8,128)(2,1)S(1)}, u32[]{:S(2)}, u32[]{:S(2)}) %collective-permute-start.6) | collective-permute-done | bytes 327712 | tf_op jit(solution)/shard_map/ppermute | solution.py:492
  49.8 0.0 collective-permute-done.5.refs_6_
  49.8 4.0 %collective-permute-done.4.refs_5_ = bf16[5,2,2,32,256]{4,3,2,1,0:T(8,128)(2,1)S(1)} collective-permute-done((bf16[5,2,2,32,256]{4,3,2,1,0:T(8,128)(2,1)S(1)}, bf16[5,2,2,32,256]{4,3,2,1,0:T(8,128)(2,1)S(1)}, u32[]{:S(2)}, u32[]{:S(2)}) %collective-permute-start.4) | collective-permute-done | bytes 327712 | tf_op jit(solution)/shard_map/ppermute | solution.py:492
  53.7 0.0 copy-done.2
  53.7 25.1 %second.1 = (bf16[2,1024,256]{2,1,0:T(8,128)(2,1)S(1)}, bf16[1024,256]{1,0:T(8,128)(2,1)S(1)}, bf16[4,2,1,32,256]{4,3,2,1,0:T(8,128)(2,1)S(1)}, bf16[4,2,1,32,25...) custom-call(s32[4,1024]{1,0:T(4,128)S(1)} %receive_places.1.meta_ref, ...), custom_call_target="tpu_custom_call" | custom-call | flops 29899999232 | bytes 1048576 | tf_op jit(solution)/shard_map/second/pallas_call | solution.py:474
  78.9 0.3 collective-permute-start.7
  79.2 4.1 %weights.1.weights_ref = bf16[2,8192,256]{2,1,0:T(8,128)(2,1)S(1)} custom-call(bf16[2,1024,768]{2,1,0:T(8,128)(2,1)S(1)} %get-tuple-element.37.rounded_ref), custom_call_target="tpu_custom_call" | custom-call | flops 6899999744 | bytes 1048576 | tf_op jit(solution)/shard_map/weights/pallas_call | solution.py:474
  83.2 0.4 collective-permute-start.8
  83.7 1.7 %collective-permute-start.9 = (bf16[4,2,1,32,256]{4,3,2,1,0:T(8,128)(2,1)S(1)}, bf16[4,2,1,32,256]{4,3,2,1,0:T(8,128)(2,1)S(1)}, u32[]{:S(2)}, u32[]{:S(2)}) collective-permute-start(bf16[4,2,1,32,256]{4,3,2,1,0:T(8,128)(2,1)S(1)} %get-tuple-element.42), channel_id=1, source_target_pairs={{0,4},{4,8},{8,12},{12,16},{16,20},{20,24},{24,28},{28,32},{32,36}... | collective-permute-start | bytes 393224 | tf_op jit(solution)/shard_map/ppermute | solution.py:492
  85.4 1.1 collective-permute-start.10
  86.5 0.0 collective-permute-done.7.refs_0_
  86.5 1.4 collective-permute-done.8.refs_1_
  88.0 0.0 collective-permute-done.9.refs_3_
  88.0 5.6 %collective-permute-done.10.refs_4_ = bf16[4,2,1,32,256]{4,3,2,1,0:T(8,128)(2,1)S(1)} collective-permute-done((bf16[4,2,1,32,256]{4,3,2,1,0:T(8,128)(2,1)S(1)}, bf16[4,2,1,32,256]{4,3,2,1,0:T(8,128)(2,1)S(1)}, u32[]{:S(2)}, u32[]{:S(2)}) %collective-permute-start.10) | collective-permute-done | bytes 131104 | tf_op jit(solution)/shard_map/ppermute | solution.py:492
  93.6 0.1 collective-permute-start.13
  93.7 0.6 collective-permute-start.12
  94.3 0.8 collective-permute-start.11
  95.1 3.2 %near_back.1.near_ref = bf16[2,1024,256]{2,1,0:T(8,128)(2,1)S(1)} custom-call(s32[4,1024]{1,0:T(4,128)S(1)} %send_places.1.meta_ref, bf16[2,1024,256]{2,1,0:T(8,128)(2,1)S(1)} %get-tuple-element.34.refs_0_), custom_call_target="tpu_custom_call" | custom-call | flops 2300000000 | bytes 1048576 | tf_op jit(solution)/shard_map/near_back/pallas_call | solution.py:474
  98.3 0.8 collective-permute-done.13.refs_7_
  99.2 1.3 collective-permute-done.12.refs_6_
  100.5 4.4 %collective-permute-done.11.refs_5_ = bf16[5,2,1,32,256]{4,3,2,1,0:T(8,128)(2,1)S(1)} collective-permute-done((bf16[5,2,1,32,256]{4,3,2,1,0:T(8,128)(2,1)S(1)}, bf16[5,2,1,32,256]{4,3,2,1,0:T(8,128)(2,1)S(1)}, u32[]{:S(2)}, u32[]{:S(2)}) %collective-permute-start.11) | collective-permute-done | bytes 163872 | tf_op jit(solution)/shard_map/ppermute | solution.py:492
  104.9 17.2 %first.1 = (bf16[2,1024,256]{2,1,0:T(8,128)(2,1)}, bf16[2048,256]{1,0:T(8,128)(2,1)S(1)}) custom-call(s32[4,1024]{1,0:T(4,128)S(1)} %send_places.1.meta_ref, bf16[2,1024,256]{2,1,0:T(8,128)(2,1)S(1)} %copy-done.1, bf16[2,1024,256]{2,1,0:T(8,128)(2,1)S(1)} %near_back.1.near_ref, bf16[2,1024,256]{2,1,0:T(8,128)(2,1)S(1)} %get-tuple-element.35.attended_ref, ...), custom_call_target="tpu_custom_call" | custom-call | flops 18400000000 | bytes 1048576 | tf_op jit(solution)/shard_map/first/pallas_call | solution.py:474
  122.1 23.0 %all_to_all.10 = bf16[128,16,256]{2,1,0:T(8,128)(2,1)S(1)} all-to-all(bf16[128,16,256]{2,1,0:T(8,128)(2,1)S(1)} %bitcast.3), channel_id=1, replica_groups=mesh['pts'=32,'grp'=4] {'pts','grp'}, dimensions={0} | all-to-all | bytes 2097152 | tf_op jit(solution)/shard_map/all_to_all | solution.py:518
  145.1 0.2 convert_reduce_fusion
  145.3 0.1 broadcast_in_dim.2
  145.3 23.0 %all_to_all.11 = bf16[128,16,256]{2,1,0:T(8,128)(2,1)S(1)} all-to-all(bf16[128,16,256]{2,1,0:T(8,128)(2,1)S(1)} %broadcast_in_dim.2), channel_id=1, replica_groups=mesh['pts'=32,'grp'=4] {'pts','grp'}, dimensions={0} | all-to-all | bytes 2097152 | tf_op jit(solution)/shard_map/all_to_all | solution.py:521
  168.4 1.4 split.1
  (20 shorter events, 0.1 us)
Async XLA Ops:
  0.6 0.7 copy-start.6
  1.3 1.3 copy-start
  1.3 1.5 copy-start.1
  1.3 1.6 copy-start.3
  1.3 1.6 copy-start.5
  3.0 33.9 %copy-start.7 = (s32[2,1024]{1,0:T(2,128)S(1)}, s32[2,1024]{1,0:T(2,128)}, u32[]{:S(2)}) copy-start(s32[2,1024]{1,0:T(2,128)} %source_ref.1) | copy-start | bytes 24580
  11.1 12.1 %collective-permute-start = (bf16[4,2,2,32,256]{4,3,2,1,0:T(8,128)(2,1)S(1)}, bf16[4,2,2,32,256]{4,3,2,1,0:T(8,128)(2,1)S(1)}, u32[]{:S(2)}, u32[]{:S(2)}) collective-permute-start(bf16[4,2,2,32,256]{4,3,2,1,0:T(8,128)(2,1)S(1)} %get-tuple-element.29), channel_id=1, source_target_pairs={{0,120},{4,124},{8,0},{12,4},{16,8},{20,12},{24,16},{28,20},{32,24... | collective-permute-start | bytes 786440 | tf_op jit(solution)/shard_map/ppermute | solution.py:492
  18.2 5.8 %collective-permute-start.1 = (bf16[4,2,2,32,256]{4,3,2,1,0:T(8,128)(2,1)S(1)}, bf16[4,2,2,32,256]{4,3,2,1,0:T(8,128)(2,1)S(1)}, u32[]{:S(2)}, u32[]{:S(2)}) collective-permute-start(bf16[4,2,2,32,256]{4,3,2,1,0:T(8,128)(2,1)S(1)} %get-tuple-element.30), channel_id=1, source_target_pairs={{0,124},{4,0},{8,4},{12,8},{16,12},{20,16},{24,20},{28,24},{32,28}... | collective-permute-start | bytes 786440 | tf_op jit(solution)/shard_map/ppermute | solution.py:492
  19.2 6.4 %collective-permute-start.2 = (bf16[4,2,2,32,256]{4,3,2,1,0:T(8,128)(2,1)S(1)}, bf16[4,2,2,32,256]{4,3,2,1,0:T(8,128)(2,1)S(1)}, u32[]{:S(2)}, u32[]{:S(2)}) collective-permute-start(bf16[4,2,2,32,256]{4,3,2,1,0:T(8,128)(2,1)S(1)} %get-tuple-element.32), channel_id=1, source_target_pairs={{0,4},{4,8},{8,12},{12,16},{16,20},{20,24},{24,28},{28,32},{32,36}... | collective-permute-start | bytes 786440 | tf_op jit(solution)/shard_map/ppermute | solution.py:492
  20.0 13.3 %collective-permute-start.3 = (bf16[4,2,2,32,256]{4,3,2,1,0:T(8,128)(2,1)S(1)}, bf16[4,2,2,32,256]{4,3,2,1,0:T(8,128)(2,1)S(1)}, u32[]{:S(2)}, u32[]{:S(2)}) collective-permute-start(bf16[4,2,2,32,256]{4,3,2,1,0:T(8,128)(2,1)S(1)} %get-tuple-element.33), channel_id=1, source_target_pairs={{0,8},{4,12},{8,16},{12,20},{16,24},{20,28},{24,32},{28,36},{32,40... | collective-permute-start | bytes 786440 | tf_op jit(solution)/shard_map/ppermute | solution.py:492
  33.2 16.5 %collective-permute-start.6 = (bf16[5,2,2,32,256]{4,3,2,1,0:T(8,128)(2,1)S(1)}, bf16[5,2,2,32,256]{4,3,2,1,0:T(8,128)(2,1)S(1)}, u32[]{:S(2)}, u32[]{:S(2)}) collective-permute-start(bf16[5,2,2,32,256]{4,3,2,1,0:T(8,128)(2,1)S(1)} %get-tuple-element.51), channel_id=1, source_target_pairs={{0,3},{1,0},{2,1},{3,2},{4,7},{5,4},{6,5},{7,6},{8,11},{9,8},{10,9... | collective-permute-start | bytes 983048 | tf_op jit(solution)/shard_map/ppermute | solution.py:492
  35.8 14.0 %collective-permute-start.5 = (bf16[5,2,2,32,256]{4,3,2,1,0:T(8,128)(2,1)S(1)}, bf16[5,2,2,32,256]{4,3,2,1,0:T(8,128)(2,1)S(1)}, u32[]{:S(2)}, u32[]{:S(2)}) collective-permute-start(bf16[5,2,2,32,256]{4,3,2,1,0:T(8,128)(2,1)S(1)} %get-tuple-element.52), channel_id=1, source_target_pairs={{0,2},{1,3},{2,0},{3,1},{4,6},{5,7},{6,4},{7,5},{8,10},{9,11},{10,... | collective-permute-start | bytes 983048 | tf_op jit(solution)/shard_map/ppermute | solution.py:492
  36.3 17.4 %collective-permute-start.4 = (bf16[5,2,2,32,256]{4,3,2,1,0:T(8,128)(2,1)S(1)}, bf16[5,2,2,32,256]{4,3,2,1,0:T(8,128)(2,1)S(1)}, u32[]{:S(2)}, u32[]{:S(2)}) collective-permute-start(bf16[5,2,2,32,256]{4,3,2,1,0:T(8,128)(2,1)S(1)} %get-tuple-element.53), channel_id=1, source_target_pairs={{0,1},{1,2},{2,3},{3,0},{4,5},{5,6},{6,7},{7,4},{8,9},{9,10},{10,1... | collective-permute-start | bytes 983048 | tf_op jit(solution)/shard_map/ppermute | solution.py:492
  38.4 15.4 %copy-start.2 = (bf16[256,768]{1,0:T(8,128)(2,1)S(1)}, bf16[256,768]{1,0:T(8,128)(2,1)}, u32[]{:S(2)}) copy-start(bf16[256,768]{1,0:T(8,128)(2,1)} %inward_ref.4) | copy-start | bytes 1179652
  38.4 15.4 %copy-start.4 = (bf16[256,256]{1,0:T(8,128)(2,1)S(1)}, bf16[256,256]{1,0:T(8,128)(2,1)}, u32[]{:S(2)}) copy-start(bf16[256,256]{1,0:T(8,128)(2,1)} %outward_ref.4) | copy-start | bytes 393220
  78.9 7.6 %collective-permute-start.7 = (bf16[4,2,1,32,256]{4,3,2,1,0:T(8,128)(2,1)S(1)}, bf16[4,2,1,32,256]{4,3,2,1,0:T(8,128)(2,1)S(1)}, u32[]{:S(2)}, u32[]{:S(2)}) collective-permute-start(bf16[4,2,1,32,256]{4,3,2,1,0:T(8,128)(2,1)S(1)} %get-tuple-element.39), channel_id=1, source_target_pairs={{0,120},{4,124},{8,0},{12,4},{16,8},{20,12},{24,16},{28,20},{32,24... | collective-permute-start | bytes 393224 | tf_op jit(solution)/shard_map/ppermute | solution.py:492
  83.2 4.7 %collective-permute-start.8 = (bf16[4,2,1,32,256]{4,3,2,1,0:T(8,128)(2,1)S(1)}, bf16[4,2,1,32,256]{4,3,2,1,0:T(8,128)(2,1)S(1)}, u32[]{:S(2)}, u32[]{:S(2)}) collective-permute-start(bf16[4,2,1,32,256]{4,3,2,1,0:T(8,128)(2,1)S(1)} %get-tuple-element.40), channel_id=1, source_target_pairs={{0,124},{4,0},{8,4},{12,8},{16,12},{20,16},{24,20},{28,24},{32,28}... | collective-permute-start | bytes 393224 | tf_op jit(solution)/shard_map/ppermute | solution.py:492
  83.7 4.3 %collective-permute-start.9 = (bf16[4,2,1,32,256]{4,3,2,1,0:T(8,128)(2,1)S(1)}, bf16[4,2,1,32,256]{4,3,2,1,0:T(8,128)(2,1)S(1)}, u32[]{:S(2)}, u32[]{:S(2)}) collective-permute-start(bf16[4,2,1,32,256]{4,3,2,1,0:T(8,128)(2,1)S(1)} %get-tuple-element.42), channel_id=1, source_target_pairs={{0,4},{4,8},{8,12},{12,16},{16,20},{20,24},{24,28},{28,32},{32,36}... | collective-permute-start | bytes 393224 | tf_op jit(solution)/shard_map/ppermute | solution.py:492
  85.4 8.2 %collective-permute-start.10 = (bf16[4,2,1,32,256]{4,3,2,1,0:T(8,128)(2,1)S(1)}, bf16[4,2,1,32,256]{4,3,2,1,0:T(8,128)(2,1)S(1)}, u32[]{:S(2)}, u32[]{:S(2)}) collective-permute-start(bf16[4,2,1,32,256]{4,3,2,1,0:T(8,128)(2,1)S(1)} %get-tuple-element.43), channel_id=1, source_target_pairs={{0,8},{4,12},{8,16},{12,20},{16,24},{20,28},{24,32},{28,36},{32,40... | collective-permute-start | bytes 393224 | tf_op jit(solution)/shard_map/ppermute | solution.py:492
  93.6 5.6 %collective-permute-start.13 = (bf16[5,2,1,32,256]{4,3,2,1,0:T(8,128)(2,1)S(1)}, bf16[5,2,1,32,256]{4,3,2,1,0:T(8,128)(2,1)S(1)}, u32[]{:S(2)}, u32[]{:S(2)}) collective-permute-start(bf16[5,2,1,32,256]{4,3,2,1,0:T(8,128)(2,1)S(1)} %get-tuple-element.66), channel_id=1, source_target_pairs={{0,3},{1,0},{2,1},{3,2},{4,7},{5,4},{6,5},{7,6},{8,11},{9,8},{10,9... | collective-permute-start | bytes 491528 | tf_op jit(solution)/shard_map/ppermute | solution.py:492
  93.7 6.8 %collective-permute-start.12 = (bf16[5,2,1,32,256]{4,3,2,1,0:T(8,128)(2,1)S(1)}, bf16[5,2,1,32,256]{4,3,2,1,0:T(8,128)(2,1)S(1)}, u32[]{:S(2)}, u32[]{:S(2)}) collective-permute-start(bf16[5,2,1,32,256]{4,3,2,1,0:T(8,128)(2,1)S(1)} %get-tuple-element.67), channel_id=1, source_target_pairs={{0,2},{1,3},{2,0},{3,1},{4,6},{5,7},{6,4},{7,5},{8,10},{9,11},{10,... | collective-permute-start | bytes 491528 | tf_op jit(solution)/shard_map/ppermute | solution.py:492
  94.3 10.6 %collective-permute-start.11 = (bf16[5,2,1,32,256]{4,3,2,1,0:T(8,128)(2,1)S(1)}, bf16[5,2,1,32,256]{4,3,2,1,0:T(8,128)(2,1)S(1)}, u32[]{:S(2)}, u32[]{:S(2)}) collective-permute-start(bf16[5,2,1,32,256]{4,3,2,1,0:T(8,128)(2,1)S(1)} %get-tuple-element.68), channel_id=1, source_target_pairs={{0,1},{1,2},{2,3},{3,0},{4,5},{5,6},{6,7},{7,4},{8,9},{9,10},{10,1... | collective-permute-start | bytes 491528 | tf_op jit(solution)/shard_map/ppermute | solution.py:492
where the time goes:
time: 170 us
  Pallas kernels  65.8 us (39%)
  blocking collectives  46 us (27%)
  waiting for transfers between devices  38.1 us (22%)
  starting transfers between devices  17.6 us (10%)
    pallas_call x9, Pallas kernels, call(): pl.pallas_call(kernel, name=name, grid=(steps,), in_specs=specs, out_spec...  65.8 us
    ppermute x14, waiting for transfers between devices, rotate(): return lax.ppermute(value, axis, pairs)  38.1 us
    all_to_all x1, blocking collectives, reduce_all(): return lax.all_to_all(spread, AXES, 0, 0, tiled=True).reshape(terms.shape)  23 us
    all_to_all x1, blocking collectives, reduce_all(): mine = lax.all_to_all(pieces, AXES, 0, 0, tiled=True)  23 us
    ppermute x14, starting transfers between devices, rotate(): return lax.ppermute(value, axis, pairs)  17.6 us
  transfers between devices with their start and end apart: 14, of which 11 were waited for; matrix products, arithmetic and copies ran while one was open for 0% of the time, Pallas kernels for 7%

commit v1 on v0

--- a/solution.py
+++ b/solution.py
@@ -617,6 +617,7 @@
         [weights_spec],
         samples,
     )
+    near, weights = lax.optimization_barrier((near, weights))
     rotated_grad, second_joined, *back_packets = call(
         second_kernel,
         "second",

time: 170 us -> 166 us (0.976)
  waiting for transfers between devices: 38.1 us -> 34.1 us
    ppermute x14, waiting for transfers between devices: 38.1 us -> 34.1 us  [rotate(): return lax.ppermute(value, axis, pairs)]
  transfers between devices with their start and end apart: 14 -> 14, of which waited for: 11 -> 10; matrix products, arithmetic and copies ran while one was open for 0% -> 0% of each run, Pallas kernels for 7% -> 8%
where the time goes in v1:
time: 166 us
  Pallas kernels  65.7 us (40%)
  blocking collectives  46 us (28%)
  waiting for transfers between devices  34.1 us (21%)
  starting transfers between devices  17.6 us (11%)
    pallas_call x9, Pallas kernels, call(): pl.pallas_call(kernel, name=name, grid=(steps,), in_specs=specs, out_spec...  65.7 us
    ppermute x14, waiting for transfers between devices, rotate(): return lax.ppermute(value, axis, pairs)  34.1 us
    all_to_all x1, blocking collectives, reduce_all(): return lax.all_to_all(spread, AXES, 0, 0, tiled=True).reshape(terms.shape)  23 us
    all_to_all x1, blocking collectives, reduce_all(): mine = lax.all_to_all(pieces, AXES, 0, 0, tiled=True)  23 us
    ppermute x14, starting transfers between devices, rotate(): return lax.ppermute(value, axis, pairs)  17.6 us
  transfers between devices with their start and end apart: 14, of which 10 were waited for; matrix products, arithmetic and copies ran while one was open for 0% of the time, Pallas kernels for 8%

profile of v1, /device:TPU:1, one launch (start us, length us, event | category | flops | bytes accessed | tf_op | source)
XLA Modules:
  0.0 165.7 jit_solution(15956701635265087745)
XLA Ops:
  0.6 0.7 copy-done.6
  1.3 1.3 send_places.1.meta_ref
  2.6 0.2 copy-done.1
  2.9 0.1 copy-done.3
  3.0 0.0 copy-done.5
  3.0 8.1 %forward.1 = (bf16[2,1024,256]{2,1,0:T(8,128)(2,1)S(1)}, bf16[2,1024,256]{2,1,0:T(8,128)(2,1)S(1)}, f32[2,1024,256]{2,1,0:T(8,128)S(1)}, bf16[2,1024,768]{2,1,0:...) custom-call(bf16[2,1024,256]{2,1,0:T(8,128)(2,1)S(1)} %copy-done.1, ...), custom_call_target="tpu_custom_call" | custom-call | flops 10350000128 | bytes 1048576 | tf_op jit(solution)/shard_map/forward/pallas_call | solution.py:474
  11.1 7.1 %collective-permute-start = (bf16[4,2,2,32,256]{4,3,2,1,0:T(8,128)(2,1)S(1)}, bf16[4,2,2,32,256]{4,3,2,1,0:T(8,128)(2,1)S(1)}, u32[]{:S(2)}, u32[]{:S(2)}) collective-permute-start(bf16[4,2,2,32,256]{4,3,2,1,0:T(8,128)(2,1)S(1)} %get-tuple-element.33), channel_id=1, source_target_pairs={{0,120},{4,124},{8,0},{12,4},{16,8},{20,12},{24,16},{28,20},{32,24... | collective-permute-start | bytes 786440 | tf_op jit(solution)/shard_map/ppermute | solution.py:492
  18.2 1.0 collective-permute-start.1
  19.2 0.8 collective-permute-start.2
  20.0 0.0 collective-permute-start.3
  20.0 4.0 %weights.1.weights_ref = bf16[2,8192,256]{2,1,0:T(8,128)(2,1)S(1)} custom-call(bf16[2,1024,768]{2,1,0:T(8,128)(2,1)S(1)} %get-tuple-element.31.rounded_ref), custom_call_target="tpu_custom_call" | custom-call | flops 6899999744 | bytes 1048576 | tf_op jit(solution)/shard_map/weights/pallas_call | solution.py:474
  24.0 0.0 collective-permute-done.refs_0_
  24.0 0.0 collective-permute-done.1.refs_1_
  24.1 1.4 collective-permute-done.2.refs_3_
  25.5 7.7 %collective-permute-done.3.refs_4_ = bf16[4,2,2,32,256]{4,3,2,1,0:T(8,128)(2,1)S(1)} collective-permute-done((bf16[4,2,2,32,256]{4,3,2,1,0:T(8,128)(2,1)S(1)}, bf16[4,2,2,32,256]{4,3,2,1,0:T(8,128)(2,1)S(1)}, u32[]{:S(2)}, u32[]{:S(2)}) %collective-permute-start.3) | collective-permute-done | bytes 262176 | tf_op jit(solution)/shard_map/ppermute | solution.py:492
  33.2 2.6 %collective-permute-start.6 = (bf16[5,2,2,32,256]{4,3,2,1,0:T(8,128)(2,1)S(1)}, bf16[5,2,2,32,256]{4,3,2,1,0:T(8,128)(2,1)S(1)}, u32[]{:S(2)}, u32[]{:S(2)}) collective-permute-start(bf16[5,2,2,32,256]{4,3,2,1,0:T(8,128)(2,1)S(1)} %get-tuple-element.55), channel_id=1, source_target_pairs={{0,3},{1,0},{2,1},{3,2},{4,7},{5,4},{6,5},{7,6},{8,11},{9,8},{10,9... | collective-permute-start | bytes 983048 | tf_op jit(solution)/shard_map/ppermute | solution.py:492
  35.8 0.5 collective-permute-start.5
  36.3 0.6 collective-permute-start.4
  36.9 0.0 copy-done.7
  36.9 1.5 receive_places.1.meta_ref
  38.4 0.0 copy-start.2
  38.4 0.0 copy-start.4
  38.4 4.0 %near_out.1.near_ref = bf16[2,1024,512]{2,1,0:T(8,128)(2,1)S(1)} custom-call(s32[4,1024]{1,0:T(4,128)S(1)} %receive_places.1.meta_ref, bf16[2,1024,256]{2,1,0:T(8,128)(2,1)S(1)} %get-tuple-element.30.refs_0_, bf16[2,1024,256]{2,1,0:T(8,128)(2,1)S(1)} %copy-done), custom_call_target="tpu_custom_call" | custom-call | flops 3449999872 | bytes 1048576 | tf_op jit(solution)/shard_map/near_out/pallas_call | solution.py:474
  42.4 7.4 %collective-permute-done.6.refs_7_ = bf16[5,2,2,32,256]{4,3,2,1,0:T(8,128)(2,1)S(1)} collective-permute-done((bf16[5,2,2,32,256]{4,3,2,1,0:T(8,128)(2,1)S(1)}, bf16[5,2,2,32,256]{4,3,2,1,0:T(8,128)(2,1)S(1)}, u32[]{:S(2)}, u32[]{:S(2)}) %collective-permute-start.6) | collective-permute-done | bytes 327712 | tf_op jit(solution)/shard_map/ppermute | solution.py:492
  49.8 0.0 collective-permute-done.5.refs_6_
  49.8 4.0 %collective-permute-done.4.refs_5_ = bf16[5,2,2,32,256]{4,3,2,1,0:T(8,128)(2,1)S(1)} collective-permute-done((bf16[5,2,2,32,256]{4,3,2,1,0:T(8,128)(2,1)S(1)}, bf16[5,2,2,32,256]{4,3,2,1,0:T(8,128)(2,1)S(1)}, u32[]{:S(2)}, u32[]{:S(2)}) %collective-permute-start.4) | collective-permute-done | bytes 327712 | tf_op jit(solution)/shard_map/ppermute | solution.py:492
  53.8 25.1 %second.1 = (bf16[2,1024,256]{2,1,0:T(8,128)(2,1)S(1)}, bf16[1024,256]{1,0:T(8,128)(2,1)S(1)}, bf16[4,2,1,32,256]{4,3,2,1,0:T(8,128)(2,1)S(1)}, bf16[4,2,1,32,25...) custom-call(s32[4,1024]{1,0:T(4,128)S(1)} %receive_places.1.meta_ref, ...), custom_call_target="tpu_custom_call" | custom-call | flops 29899999232 | bytes 1048576 | tf_op jit(solution)/shard_map/second/pallas_call | solution.py:474
  78.8 0.3 collective-permute-start.7
  79.2 0.5 collective-permute-start.8
  79.6 1.6 collective-permute-start.9
  81.2 1.2 collective-permute-start.10
  82.4 1.5 collective-permute-done.7.refs_0_
  83.8 2.2 %collective-permute-done.8.refs_1_ = bf16[4,2,1,32,256]{4,3,2,1,0:T(8,128)(2,1)S(1)} collective-permute-done((bf16[4,2,1,32,256]{4,3,2,1,0:T(8,128)(2,1)S(1)}, bf16[4,2,1,32,256]{4,3,2,1,0:T(8,128)(2,1)S(1)}, u32[]{:S(2)}, u32[]{:S(2)}) %collective-permute-start.8) | collective-permute-done | bytes 131104 | tf_op jit(solution)/shard_map/ppermute | solution.py:492
  86.1 0.0 collective-permute-done.9.refs_3_
  86.1 3.4 %collective-permute-done.10.refs_4_ = bf16[4,2,1,32,256]{4,3,2,1,0:T(8,128)(2,1)S(1)} collective-permute-done((bf16[4,2,1,32,256]{4,3,2,1,0:T(8,128)(2,1)S(1)}, bf16[4,2,1,32,256]{4,3,2,1,0:T(8,128)(2,1)S(1)}, u32[]{:S(2)}, u32[]{:S(2)}) %collective-permute-start.10) | collective-permute-done | bytes 131104 | tf_op jit(solution)/shard_map/ppermute | solution.py:492
  89.5 0.1 collective-permute-start.13
  89.7 0.6 collective-permute-start.12
  90.2 0.8 collective-permute-start.11
  91.1 3.2 %near_back.1.near_ref = bf16[2,1024,256]{2,1,0:T(8,128)(2,1)S(1)} custom-call(s32[4,1024]{1,0:T(4,128)S(1)} %send_places.1.meta_ref, bf16[2,1024,256]{2,1,0:T(8,128)(2,1)S(1)} %get-tuple-element.38.refs_0_), custom_call_target="tpu_custom_call" | custom-call | flops 2300000000 | bytes 1048576 | tf_op jit(solution)/shard_map/near_back/pallas_call | solution.py:474
  94.3 0.8 collective-permute-done.13.refs_7_
  95.1 1.3 collective-permute-done.12.refs_6_
  96.4 4.4 %collective-permute-done.11.refs_5_ = bf16[5,2,1,32,256]{4,3,2,1,0:T(8,128)(2,1)S(1)} collective-permute-done((bf16[5,2,1,32,256]{4,3,2,1,0:T(8,128)(2,1)S(1)}, bf16[5,2,1,32,256]{4,3,2,1,0:T(8,128)(2,1)S(1)}, u32[]{:S(2)}, u32[]{:S(2)}) %collective-permute-start.11) | collective-permute-done | bytes 163872 | tf_op jit(solution)/shard_map/ppermute | solution.py:492
  100.8 17.1 %first.1 = (bf16[2,1024,256]{2,1,0:T(8,128)(2,1)}, bf16[2048,256]{1,0:T(8,128)(2,1)S(1)}) custom-call(s32[4,1024]{1,0:T(4,128)S(1)} %send_places.1.meta_ref, bf16[2,1024,256]{2,1,0:T(8,128)(2,1)S(1)} %copy-done.1, bf16[2,1024,256]{2,1,0:T(8,128)(2,1)S(1)} %near_back.1.near_ref, bf16[2,1024,256]{2,1,0:T(8,128)(2,1)S(1)} %get-tuple-element.39.attended_ref, ...), custom_call_target="tpu_custom_call" | custom-call | flops 18400000000 | bytes 1048576 | tf_op jit(solution)/shard_map/first/pallas_call | solution.py:474
  118.0 23.0 %all_to_all.10 = bf16[128,16,256]{2,1,0:T(8,128)(2,1)S(1)} all-to-all(bf16[128,16,256]{2,1,0:T(8,128)(2,1)S(1)} %bitcast.3), channel_id=1, replica_groups=mesh['pts'=32,'grp'=4] {'pts','grp'}, dimensions={0} | all-to-all | bytes 2097152 | tf_op jit(solution)/shard_map/all_to_all | solution.py:518
  141.0 0.2 convert_reduce_fusion
  141.2 0.1 broadcast_in_dim.2
  141.2 23.0 %all_to_all.11 = bf16[128,16,256]{2,1,0:T(8,128)(2,1)S(1)} all-to-all(bf16[128,16,256]{2,1,0:T(8,128)(2,1)S(1)} %broadcast_in_dim.2), channel_id=1, replica_groups=mesh['pts'=32,'grp'=4] {'pts','grp'}, dimensions={0} | all-to-all | bytes 2097152 | tf_op jit(solution)/shard_map/all_to_all | solution.py:521
  164.3 1.4 split.1
  (20 shorter events, 0.1 us)
Async XLA Ops:
  0.6 0.7 copy-start.6
  1.3 1.3 copy-start
  1.3 1.5 copy-start.1
  1.3 1.6 copy-start.3
  1.3 1.6 copy-start.5
  11.1 12.9 %collective-permute-start = (bf16[4,2,2,32,256]{4,3,2,1,0:T(8,128)(2,1)S(1)}, bf16[4,2,2,32,256]{4,3,2,1,0:T(8,128)(2,1)S(1)}, u32[]{:S(2)}, u32[]{:S(2)}) collective-permute-start(bf16[4,2,2,32,256]{4,3,2,1,0:T(8,128)(2,1)S(1)} %get-tuple-element.33), channel_id=1, source_target_pairs={{0,120},{4,124},{8,0},{12,4},{16,8},{20,12},{24,16},{28,20},{32,24... | collective-permute-start | bytes 786440 | tf_op jit(solution)/shard_map/ppermute | solution.py:492
  18.2 5.8 %collective-permute-start.1 = (bf16[4,2,2,32,256]{4,3,2,1,0:T(8,128)(2,1)S(1)}, bf16[4,2,2,32,256]{4,3,2,1,0:T(8,128)(2,1)S(1)}, u32[]{:S(2)}, u32[]{:S(2)}) collective-permute-start(bf16[4,2,2,32,256]{4,3,2,1,0:T(8,128)(2,1)S(1)} %get-tuple-element.34), channel_id=1, source_target_pairs={{0,124},{4,0},{8,4},{12,8},{16,12},{20,16},{24,20},{28,24},{32,28}... | collective-permute-start | bytes 786440 | tf_op jit(solution)/shard_map/ppermute | solution.py:492
  19.2 6.4 %collective-permute-start.2 = (bf16[4,2,2,32,256]{4,3,2,1,0:T(8,128)(2,1)S(1)}, bf16[4,2,2,32,256]{4,3,2,1,0:T(8,128)(2,1)S(1)}, u32[]{:S(2)}, u32[]{:S(2)}) collective-permute-start(bf16[4,2,2,32,256]{4,3,2,1,0:T(8,128)(2,1)S(1)} %get-tuple-element.36), channel_id=1, source_target_pairs={{0,4},{4,8},{8,12},{12,16},{16,20},{20,24},{24,28},{28,32},{32,36}... | collective-permute-start | bytes 786440 | tf_op jit(solution)/shard_map/ppermute | solution.py:492
  20.0 13.3 %collective-permute-start.3 = (bf16[4,2,2,32,256]{4,3,2,1,0:T(8,128)(2,1)S(1)}, bf16[4,2,2,32,256]{4,3,2,1,0:T(8,128)(2,1)S(1)}, u32[]{:S(2)}, u32[]{:S(2)}) collective-permute-start(bf16[4,2,2,32,256]{4,3,2,1,0:T(8,128)(2,1)S(1)} %get-tuple-element.37), channel_id=1, source_target_pairs={{0,8},{4,12},{8,16},{12,20},{16,24},{20,28},{24,32},{28,36},{32,40... | collective-permute-start | bytes 786440 | tf_op jit(solution)/shard_map/ppermute | solution.py:492
  20.0 16.9 %copy-start.7 = (s32[2,1024]{1,0:T(2,128)S(1)}, s32[2,1024]{1,0:T(2,128)}, u32[]{:S(2)}) copy-start(s32[2,1024]{1,0:T(2,128)} %source_ref.1) | copy-start | bytes 24580
  33.2 16.5 %collective-permute-start.6 = (bf16[5,2,2,32,256]{4,3,2,1,0:T(8,128)(2,1)S(1)}, bf16[5,2,2,32,256]{4,3,2,1,0:T(8,128)(2,1)S(1)}, u32[]{:S(2)}, u32[]{:S(2)}) collective-permute-start(bf16[5,2,2,32,256]{4,3,2,1,0:T(8,128)(2,1)S(1)} %get-tuple-element.55), channel_id=1, source_target_pairs={{0,3},{1,0},{2,1},{3,2},{4,7},{5,4},{6,5},{7,6},{8,11},{9,8},{10,9... | collective-permute-start | bytes 983048 | tf_op jit(solution)/shard_map/ppermute | solution.py:492
  35.8 14.0 %collective-permute-start.5 = (bf16[5,2,2,32,256]{4,3,2,1,0:T(8,128)(2,1)S(1)}, bf16[5,2,2,32,256]{4,3,2,1,0:T(8,128)(2,1)S(1)}, u32[]{:S(2)}, u32[]{:S(2)}) collective-permute-start(bf16[5,2,2,32,256]{4,3,2,1,0:T(8,128)(2,1)S(1)} %get-tuple-element.56), channel_id=1, source_target_pairs={{0,2},{1,3},{2,0},{3,1},{4,6},{5,7},{6,4},{7,5},{8,10},{9,11},{10,... | collective-permute-start | bytes 983048 | tf_op jit(solution)/shard_map/ppermute | solution.py:492
  36.3 17.4 %collective-permute-start.4 = (bf16[5,2,2,32,256]{4,3,2,1,0:T(8,128)(2,1)S(1)}, bf16[5,2,2,32,256]{4,3,2,1,0:T(8,128)(2,1)S(1)}, u32[]{:S(2)}, u32[]{:S(2)}) collective-permute-start(bf16[5,2,2,32,256]{4,3,2,1,0:T(8,128)(2,1)S(1)} %get-tuple-element.57), channel_id=1, source_target_pairs={{0,1},{1,2},{2,3},{3,0},{4,5},{5,6},{6,7},{7,4},{8,9},{9,10},{10,1... | collective-permute-start | bytes 983048 | tf_op jit(solution)/shard_map/ppermute | solution.py:492
  38.4 15.4 %copy-start.2 = (bf16[256,768]{1,0:T(8,128)(2,1)S(1)}, bf16[256,768]{1,0:T(8,128)(2,1)}, u32[]{:S(2)}) copy-start(bf16[256,768]{1,0:T(8,128)(2,1)} %inward_ref.4) | copy-start | bytes 1179652
  38.4 15.4 %copy-start.4 = (bf16[256,256]{1,0:T(8,128)(2,1)S(1)}, bf16[256,256]{1,0:T(8,128)(2,1)}, u32[]{:S(2)}) copy-start(bf16[256,256]{1,0:T(8,128)(2,1)} %outward_ref.4) | copy-start | bytes 393220
  78.8 5.0 %collective-permute-start.7 = (bf16[4,2,1,32,256]{4,3,2,1,0:T(8,128)(2,1)S(1)}, bf16[4,2,1,32,256]{4,3,2,1,0:T(8,128)(2,1)S(1)}, u32[]{:S(2)}, u32[]{:S(2)}) collective-permute-start(bf16[4,2,1,32,256]{4,3,2,1,0:T(8,128)(2,1)S(1)} %get-tuple-element.43), channel_id=1, source_target_pairs={{0,120},{4,124},{8,0},{12,4},{16,8},{20,12},{24,16},{28,20},{32,24... | collective-permute-start | bytes 393224 | tf_op jit(solution)/shard_map/ppermute | solution.py:492
  79.2 6.9 %collective-permute-start.8 = (bf16[4,2,1,32,256]{4,3,2,1,0:T(8,128)(2,1)S(1)}, bf16[4,2,1,32,256]{4,3,2,1,0:T(8,128)(2,1)S(1)}, u32[]{:S(2)}, u32[]{:S(2)}) collective-permute-start(bf16[4,2,1,32,256]{4,3,2,1,0:T(8,128)(2,1)S(1)} %get-tuple-element.44), channel_id=1, source_target_pairs={{0,124},{4,0},{8,4},{12,8},{16,12},{20,16},{24,20},{28,24},{32,28}... | collective-permute-start | bytes 393224 | tf_op jit(solution)/shard_map/ppermute | solution.py:492
  79.6 6.5 %collective-permute-start.9 = (bf16[4,2,1,32,256]{4,3,2,1,0:T(8,128)(2,1)S(1)}, bf16[4,2,1,32,256]{4,3,2,1,0:T(8,128)(2,1)S(1)}, u32[]{:S(2)}, u32[]{:S(2)}) collective-permute-start(bf16[4,2,1,32,256]{4,3,2,1,0:T(8,128)(2,1)S(1)} %get-tuple-element.46), channel_id=1, source_target_pairs={{0,4},{4,8},{8,12},{12,16},{16,20},{20,24},{24,28},{28,32},{32,36}... | collective-permute-start | bytes 393224 | tf_op jit(solution)/shard_map/ppermute | solution.py:492
  81.2 8.4 %collective-permute-start.10 = (bf16[4,2,1,32,256]{4,3,2,1,0:T(8,128)(2,1)S(1)}, bf16[4,2,1,32,256]{4,3,2,1,0:T(8,128)(2,1)S(1)}, u32[]{:S(2)}, u32[]{:S(2)}) collective-permute-start(bf16[4,2,1,32,256]{4,3,2,1,0:T(8,128)(2,1)S(1)} %get-tuple-element.47), channel_id=1, source_target_pairs={{0,8},{4,12},{8,16},{12,20},{16,24},{20,28},{24,32},{28,36},{32,40... | collective-permute-start | bytes 393224 | tf_op jit(solution)/shard_map/ppermute | solution.py:492
  89.5 5.6 %collective-permute-start.13 = (bf16[5,2,1,32,256]{4,3,2,1,0:T(8,128)(2,1)S(1)}, bf16[5,2,1,32,256]{4,3,2,1,0:T(8,128)(2,1)S(1)}, u32[]{:S(2)}, u32[]{:S(2)}) collective-permute-start(bf16[5,2,1,32,256]{4,3,2,1,0:T(8,128)(2,1)S(1)} %get-tuple-element.70), channel_id=1, source_target_pairs={{0,3},{1,0},{2,1},{3,2},{4,7},{5,4},{6,5},{7,6},{8,11},{9,8},{10,9... | collective-permute-start | bytes 491528 | tf_op jit(solution)/shard_map/ppermute | solution.py:492
  89.7 6.8 %collective-permute-start.12 = (bf16[5,2,1,32,256]{4,3,2,1,0:T(8,128)(2,1)S(1)}, bf16[5,2,1,32,256]{4,3,2,1,0:T(8,128)(2,1)S(1)}, u32[]{:S(2)}, u32[]{:S(2)}) collective-permute-start(bf16[5,2,1,32,256]{4,3,2,1,0:T(8,128)(2,1)S(1)} %get-tuple-element.71), channel_id=1, source_target_pairs={{0,2},{1,3},{2,0},{3,1},{4,6},{5,7},{6,4},{7,5},{8,10},{9,11},{10,... | collective-permute-start | bytes 491528 | tf_op jit(solution)/shard_map/ppermute | solution.py:492
  90.2 10.6 %collective-permute-start.11 = (bf16[5,2,1,32,256]{4,3,2,1,0:T(8,128)(2,1)S(1)}, bf16[5,2,1,32,256]{4,3,2,1,0:T(8,128)(2,1)S(1)}, u32[]{:S(2)}, u32[]{:S(2)}) collective-permute-start(bf16[5,2,1,32,256]{4,3,2,1,0:T(8,128)(2,1)S(1)} %get-tuple-element.72), channel_id=1, source_target_pairs={{0,1},{1,2},{2,3},{3,0},{4,5},{5,6},{6,7},{7,4},{8,9},{9,10},{10,1... | collective-permute-start | bytes 491528 | tf_op jit(solution)/shard_map/ppermute | solution.py:492

commit v2 on v1

--- a/solution.py
+++ b/solution.py
@@ -493,7 +493,10 @@
 
 
 def hop_stage(packets):
-    return [p if hop == 0 else rotate(p, "pts", hop) for hop, p in zip(HOPS, packets)]
+    moved = dict(zip(HOPS, packets))
+    for hop in sorted((hop for hop in HOPS if hop != 0), key=lambda hop: (-abs(hop), hop)):
+        moved[hop] = rotate(moved[hop], "pts", hop)
+    return [moved[hop] for hop in HOPS]
 
 
 def restack(moved):

time: 166 us -> 166 us (level)
  no operation moved by 1% of the time
where the time goes in v2:
time: 166 us
  Pallas kernels  65.7 us (40%)
  blocking collectives  46 us (28%)
  waiting for transfers between devices  34.1 us (21%)
  starting transfers between devices  17.6 us (11%)
    pallas_call x9, Pallas kernels, call(): pl.pallas_call(kernel, name=name, grid=(steps,), in_specs=specs, out_spec...  65.7 us
    ppermute x14, waiting for transfers between devices, rotate(): return lax.ppermute(value, axis, pairs)  34.1 us
    all_to_all x1, blocking collectives, reduce_all(): return lax.all_to_all(spread, AXES, 0, 0, tiled=True).reshape(terms.shape)  23 us
    all_to_all x1, blocking collectives, reduce_all(): mine = lax.all_to_all(pieces, AXES, 0, 0, tiled=True)  23 us
    ppermute x14, starting transfers between devices, rotate(): return lax.ppermute(value, axis, pairs)  17.6 us
  transfers between devices with their start and end apart: 14, of which 10 were waited for; matrix products, arithmetic and copies ran while one was open for 0% of the time, Pallas kernels for 8%

profile of v2, /device:TPU:1, one launch (start us, length us, event | category | flops | bytes accessed | tf_op | source)
XLA Modules:
  0.0 165.7 jit_solution(15956701635265087745)
XLA Ops:
  0.6 0.7 copy-done.6
  1.3 1.3 send_places.1.meta_ref
  2.6 0.2 copy-done.1
  2.9 0.1 copy-done.3
  3.0 0.0 copy-done.5
  3.0 8.1 %forward.1 = (bf16[2,1024,256]{2,1,0:T(8,128)(2,1)S(1)}, bf16[2,1024,256]{2,1,0:T(8,128)(2,1)S(1)}, f32[2,1024,256]{2,1,0:T(8,128)S(1)}, bf16[2,1024,768]{2,1,0:...) custom-call(bf16[2,1024,256]{2,1,0:T(8,128)(2,1)S(1)} %copy-done.1, ...), custom_call_target="tpu_custom_call" | custom-call | flops 10350000128 | bytes 1048576 | tf_op jit(solution)/shard_map/forward/pallas_call | solution.py:474
  11.1 7.1 %collective-permute-start = (bf16[4,2,2,32,256]{4,3,2,1,0:T(8,128)(2,1)S(1)}, bf16[4,2,2,32,256]{4,3,2,1,0:T(8,128)(2,1)S(1)}, u32[]{:S(2)}, u32[]{:S(2)}) collective-permute-start(bf16[4,2,2,32,256]{4,3,2,1,0:T(8,128)(2,1)S(1)} %get-tuple-element.33), channel_id=1, source_target_pairs={{0,120},{4,124},{8,0},{12,4},{16,8},{20,12},{24,16},{28,20},{32,24... | collective-permute-start | bytes 786440 | tf_op jit(solution)/shard_map/ppermute | solution.py:492
  18.2 1.0 collective-permute-start.1
  19.2 0.8 collective-permute-start.2
  20.0 0.0 collective-permute-start.3
  20.0 4.0 %weights.1.weights_ref = bf16[2,8192,256]{2,1,0:T(8,128)(2,1)S(1)} custom-call(bf16[2,1024,768]{2,1,0:T(8,128)(2,1)S(1)} %get-tuple-element.31.rounded_ref), custom_call_target="tpu_custom_call" | custom-call | flops 6899999744 | bytes 1048576 | tf_op jit(solution)/shard_map/weights/pallas_call | solution.py:474
  24.0 0.0 collective-permute-done.refs_0_
  24.0 0.0 collective-permute-done.1.refs_1_
  24.1 1.4 collective-permute-done.2.refs_3_
  25.5 7.7 %collective-permute-done.3.refs_4_ = bf16[4,2,2,32,256]{4,3,2,1,0:T(8,128)(2,1)S(1)} collective-permute-done((bf16[4,2,2,32,256]{4,3,2,1,0:T(8,128)(2,1)S(1)}, bf16[4,2,2,32,256]{4,3,2,1,0:T(8,128)(2,1)S(1)}, u32[]{:S(2)}, u32[]{:S(2)}) %collective-permute-start.3) | collective-permute-done | bytes 262176 | tf_op jit(solution)/shard_map/ppermute | solution.py:492
  33.2 2.6 %collective-permute-start.6 = (bf16[5,2,2,32,256]{4,3,2,1,0:T(8,128)(2,1)S(1)}, bf16[5,2,2,32,256]{4,3,2,1,0:T(8,128)(2,1)S(1)}, u32[]{:S(2)}, u32[]{:S(2)}) collective-permute-start(bf16[5,2,2,32,256]{4,3,2,1,0:T(8,128)(2,1)S(1)} %get-tuple-element.55), channel_id=1, source_target_pairs={{0,3},{1,0},{2,1},{3,2},{4,7},{5,4},{6,5},{7,6},{8,11},{9,8},{10,9... | collective-permute-start | bytes 983048 | tf_op jit(solution)/shard_map/ppermute | solution.py:492
  35.8 0.5 collective-permute-start.5
  36.3 0.6 collective-permute-start.4
  36.9 0.0 copy-done.7
  36.9 1.5 receive_places.1.meta_ref
  38.4 0.0 copy-start.2
  38.4 0.0 copy-start.4
  38.4 4.0 %near_out.1.near_ref = bf16[2,1024,512]{2,1,0:T(8,128)(2,1)S(1)} custom-call(s32[4,1024]{1,0:T(4,128)S(1)} %receive_places.1.meta_ref, bf16[2,1024,256]{2,1,0:T(8,128)(2,1)S(1)} %get-tuple-element.30.refs_0_, bf16[2,1024,256]{2,1,0:T(8,128)(2,1)S(1)} %copy-done), custom_call_target="tpu_custom_call" | custom-call | flops 3449999872 | bytes 1048576 | tf_op jit(solution)/shard_map/near_out/pallas_call | solution.py:474
  42.4 7.4 %collective-permute-done.6.refs_7_ = bf16[5,2,2,32,256]{4,3,2,1,0:T(8,128)(2,1)S(1)} collective-permute-done((bf16[5,2,2,32,256]{4,3,2,1,0:T(8,128)(2,1)S(1)}, bf16[5,2,2,32,256]{4,3,2,1,0:T(8,128)(2,1)S(1)}, u32[]{:S(2)}, u32[]{:S(2)}) %collective-permute-start.6) | collective-permute-done | bytes 327712 | tf_op jit(solution)/shard_map/ppermute | solution.py:492
  49.8 0.0 collective-permute-done.5.refs_6_
  49.8 4.0 %collective-permute-done.4.refs_5_ = bf16[5,2,2,32,256]{4,3,2,1,0:T(8,128)(2,1)S(1)} collective-permute-done((bf16[5,2,2,32,256]{4,3,2,1,0:T(8,128)(2,1)S(1)}, bf16[5,2,2,32,256]{4,3,2,1,0:T(8,128)(2,1)S(1)}, u32[]{:S(2)}, u32[]{:S(2)}) %collective-permute-start.4) | collective-permute-done | bytes 327712 | tf_op jit(solution)/shard_map/ppermute | solution.py:492
  53.8 25.1 %second.1 = (bf16[2,1024,256]{2,1,0:T(8,128)(2,1)S(1)}, bf16[1024,256]{1,0:T(8,128)(2,1)S(1)}, bf16[4,2,1,32,256]{4,3,2,1,0:T(8,128)(2,1)S(1)}, bf16[4,2,1,32,25...) custom-call(s32[4,1024]{1,0:T(4,128)S(1)} %receive_places.1.meta_ref, ...), custom_call_target="tpu_custom_call" | custom-call | flops 29899999232 | bytes 1048576 | tf_op jit(solution)/shard_map/second/pallas_call | solution.py:474
  78.8 0.3 collective-permute-start.7
  79.2 0.5 collective-permute-start.8
  79.6 1.6 collective-permute-start.9
  81.2 1.2 collective-permute-start.10
  82.4 1.5 collective-permute-done.7.refs_0_
  83.8 2.2 %collective-permute-done.8.refs_1_ = bf16[4,2,1,32,256]{4,3,2,1,0:T(8,128)(2,1)S(1)} collective-permute-done((bf16[4,2,1,32,256]{4,3,2,1,0:T(8,128)(2,1)S(1)}, bf16[4,2,1,32,256]{4,3,2,1,0:T(8,128)(2,1)S(1)}, u32[]{:S(2)}, u32[]{:S(2)}) %collective-permute-start.8) | collective-permute-done | bytes 131104 | tf_op jit(solution)/shard_map/ppermute | solution.py:492
  86.1 0.0 collective-permute-done.9.refs_3_
  86.1 3.4 %collective-permute-done.10.refs_4_ = bf16[4,2,1,32,256]{4,3,2,1,0:T(8,128)(2,1)S(1)} collective-permute-done((bf16[4,2,1,32,256]{4,3,2,1,0:T(8,128)(2,1)S(1)}, bf16[4,2,1,32,256]{4,3,2,1,0:T(8,128)(2,1)S(1)}, u32[]{:S(2)}, u32[]{:S(2)}) %collective-permute-start.10) | collective-permute-done | bytes 131104 | tf_op jit(solution)/shard_map/ppermute | solution.py:492
  89.5 0.1 collective-permute-start.13
  89.7 0.6 collective-permute-start.12
  90.2 0.8 collective-permute-start.11
  91.1 3.2 %near_back.1.near_ref = bf16[2,1024,256]{2,1,0:T(8,128)(2,1)S(1)} custom-call(s32[4,1024]{1,0:T(4,128)S(1)} %send_places.1.meta_ref, bf16[2,1024,256]{2,1,0:T(8,128)(2,1)S(1)} %get-tuple-element.38.refs_0_), custom_call_target="tpu_custom_call" | custom-call | flops 2300000000 | bytes 1048576 | tf_op jit(solution)/shard_map/near_back/pallas_call | solution.py:474
  94.3 0.8 collective-permute-done.13.refs_7_
  95.1 1.3 collective-permute-done.12.refs_6_
  96.4 4.4 %collective-permute-done.11.refs_5_ = bf16[5,2,1,32,256]{4,3,2,1,0:T(8,128)(2,1)S(1)} collective-permute-done((bf16[5,2,1,32,256]{4,3,2,1,0:T(8,128)(2,1)S(1)}, bf16[5,2,1,32,256]{4,3,2,1,0:T(8,128)(2,1)S(1)}, u32[]{:S(2)}, u32[]{:S(2)}) %collective-permute-start.11) | collective-permute-done | bytes 163872 | tf_op jit(solution)/shard_map/ppermute | solution.py:492
  100.8 17.1 %first.1 = (bf16[2,1024,256]{2,1,0:T(8,128)(2,1)}, bf16[2048,256]{1,0:T(8,128)(2,1)S(1)}) custom-call(s32[4,1024]{1,0:T(4,128)S(1)} %send_places.1.meta_ref, bf16[2,1024,256]{2,1,0:T(8,128)(2,1)S(1)} %copy-done.1, bf16[2,1024,256]{2,1,0:T(8,128)(2,1)S(1)} %near_back.1.near_ref, bf16[2,1024,256]{2,1,0:T(8,128)(2,1)S(1)} %get-tuple-element.39.attended_ref, ...), custom_call_target="tpu_custom_call" | custom-call | flops 18400000000 | bytes 1048576 | tf_op jit(solution)/shard_map/first/pallas_call | solution.py:474
  118.0 23.0 %all_to_all.10 = bf16[128,16,256]{2,1,0:T(8,128)(2,1)S(1)} all-to-all(bf16[128,16,256]{2,1,0:T(8,128)(2,1)S(1)} %bitcast.3), channel_id=1, replica_groups=mesh['pts'=32,'grp'=4] {'pts','grp'}, dimensions={0} | all-to-all | bytes 2097152 | tf_op jit(solution)/shard_map/all_to_all | solution.py:521
  141.0 0.2 convert_reduce_fusion
  141.2 0.1 broadcast_in_dim.2
  141.2 23.0 %all_to_all.11 = bf16[128,16,256]{2,1,0:T(8,128)(2,1)S(1)} all-to-all(bf16[128,16,256]{2,1,0:T(8,128)(2,1)S(1)} %broadcast_in_dim.2), channel_id=1, replica_groups=mesh['pts'=32,'grp'=4] {'pts','grp'}, dimensions={0} | all-to-all | bytes 2097152 | tf_op jit(solution)/shard_map/all_to_all | solution.py:524
  164.3 1.4 split.1
  (20 shorter events, 0.1 us)
Async XLA Ops:
  0.6 0.7 copy-start.6
  1.3 1.3 copy-start
  1.3 1.5 copy-start.1
  1.3 1.6 copy-start.3
  1.3 1.6 copy-start.5
  11.1 12.9 %collective-permute-start = (bf16[4,2,2,32,256]{4,3,2,1,0:T(8,128)(2,1)S(1)}, bf16[4,2,2,32,256]{4,3,2,1,0:T(8,128)(2,1)S(1)}, u32[]{:S(2)}, u32[]{:S(2)}) collective-permute-start(bf16[4,2,2,32,256]{4,3,2,1,0:T(8,128)(2,1)S(1)} %get-tuple-element.33), channel_id=1, source_target_pairs={{0,120},{4,124},{8,0},{12,4},{16,8},{20,12},{24,16},{28,20},{32,24... | collective-permute-start | bytes 786440 | tf_op jit(solution)/shard_map/ppermute | solution.py:492
  18.2 5.8 %collective-permute-start.1 = (bf16[4,2,2,32,256]{4,3,2,1,0:T(8,128)(2,1)S(1)}, bf16[4,2,2,32,256]{4,3,2,1,0:T(8,128)(2,1)S(1)}, u32[]{:S(2)}, u32[]{:S(2)}) collective-permute-start(bf16[4,2,2,32,256]{4,3,2,1,0:T(8,128)(2,1)S(1)} %get-tuple-element.34), channel_id=1, source_target_pairs={{0,124},{4,0},{8,4},{12,8},{16,12},{20,16},{24,20},{28,24},{32,28}... | collective-permute-start | bytes 786440 | tf_op jit(solution)/shard_map/ppermute | solution.py:492
  19.2 6.4 %collective-permute-start.2 = (bf16[4,2,2,32,256]{4,3,2,1,0:T(8,128)(2,1)S(1)}, bf16[4,2,2,32,256]{4,3,2,1,0:T(8,128)(2,1)S(1)}, u32[]{:S(2)}, u32[]{:S(2)}) collective-permute-start(bf16[4,2,2,32,256]{4,3,2,1,0:T(8,128)(2,1)S(1)} %get-tuple-element.36), channel_id=1, source_target_pairs={{0,4},{4,8},{8,12},{12,16},{16,20},{20,24},{24,28},{28,32},{32,36}... | collective-permute-start | bytes 786440 | tf_op jit(solution)/shard_map/ppermute | solution.py:492
  20.0 13.3 %collective-permute-start.3 = (bf16[4,2,2,32,256]{4,3,2,1,0:T(8,128)(2,1)S(1)}, bf16[4,2,2,32,256]{4,3,2,1,0:T(8,128)(2,1)S(1)}, u32[]{:S(2)}, u32[]{:S(2)}) collective-permute-start(bf16[4,2,2,32,256]{4,3,2,1,0:T(8,128)(2,1)S(1)} %get-tuple-element.37), channel_id=1, source_target_pairs={{0,8},{4,12},{8,16},{12,20},{16,24},{20,28},{24,32},{28,36},{32,40... | collective-permute-start | bytes 786440 | tf_op jit(solution)/shard_map/ppermute | solution.py:492
  20.0 16.9 %copy-start.7 = (s32[2,1024]{1,0:T(2,128)S(1)}, s32[2,1024]{1,0:T(2,128)}, u32[]{:S(2)}) copy-start(s32[2,1024]{1,0:T(2,128)} %source_ref.1) | copy-start | bytes 24580
  33.2 16.5 %collective-permute-start.6 = (bf16[5,2,2,32,256]{4,3,2,1,0:T(8,128)(2,1)S(1)}, bf16[5,2,2,32,256]{4,3,2,1,0:T(8,128)(2,1)S(1)}, u32[]{:S(2)}, u32[]{:S(2)}) collective-permute-start(bf16[5,2,2,32,256]{4,3,2,1,0:T(8,128)(2,1)S(1)} %get-tuple-element.55), channel_id=1, source_target_pairs={{0,3},{1,0},{2,1},{3,2},{4,7},{5,4},{6,5},{7,6},{8,11},{9,8},{10,9... | collective-permute-start | bytes 983048 | tf_op jit(solution)/shard_map/ppermute | solution.py:492
  35.8 14.0 %collective-permute-start.5 = (bf16[5,2,2,32,256]{4,3,2,1,0:T(8,128)(2,1)S(1)}, bf16[5,2,2,32,256]{4,3,2,1,0:T(8,128)(2,1)S(1)}, u32[]{:S(2)}, u32[]{:S(2)}) collective-permute-start(bf16[5,2,2,32,256]{4,3,2,1,0:T(8,128)(2,1)S(1)} %get-tuple-element.56), channel_id=1, source_target_pairs={{0,2},{1,3},{2,0},{3,1},{4,6},{5,7},{6,4},{7,5},{8,10},{9,11},{10,... | collective-permute-start | bytes 983048 | tf_op jit(solution)/shard_map/ppermute | solution.py:492
  36.3 17.4 %collective-permute-start.4 = (bf16[5,2,2,32,256]{4,3,2,1,0:T(8,128)(2,1)S(1)}, bf16[5,2,2,32,256]{4,3,2,1,0:T(8,128)(2,1)S(1)}, u32[]{:S(2)}, u32[]{:S(2)}) collective-permute-start(bf16[5,2,2,32,256]{4,3,2,1,0:T(8,128)(2,1)S(1)} %get-tuple-element.57), channel_id=1, source_target_pairs={{0,1},{1,2},{2,3},{3,0},{4,5},{5,6},{6,7},{7,4},{8,9},{9,10},{10,1... | collective-permute-start | bytes 983048 | tf_op jit(solution)/shard_map/ppermute | solution.py:492
  38.4 15.4 %copy-start.2 = (bf16[256,768]{1,0:T(8,128)(2,1)S(1)}, bf16[256,768]{1,0:T(8,128)(2,1)}, u32[]{:S(2)}) copy-start(bf16[256,768]{1,0:T(8,128)(2,1)} %inward_ref.4) | copy-start | bytes 1179652
  38.4 15.4 %copy-start.4 = (bf16[256,256]{1,0:T(8,128)(2,1)S(1)}, bf16[256,256]{1,0:T(8,128)(2,1)}, u32[]{:S(2)}) copy-start(bf16[256,256]{1,0:T(8,128)(2,1)} %outward_ref.4) | copy-start | bytes 393220
  78.8 5.0 %collective-permute-start.7 = (bf16[4,2,1,32,256]{4,3,2,1,0:T(8,128)(2,1)S(1)}, bf16[4,2,1,32,256]{4,3,2,1,0:T(8,128)(2,1)S(1)}, u32[]{:S(2)}, u32[]{:S(2)}) collective-permute-start(bf16[4,2,1,32,256]{4,3,2,1,0:T(8,128)(2,1)S(1)} %get-tuple-element.43), channel_id=1, source_target_pairs={{0,120},{4,124},{8,0},{12,4},{16,8},{20,12},{24,16},{28,20},{32,24... | collective-permute-start | bytes 393224 | tf_op jit(solution)/shard_map/ppermute | solution.py:492
  79.2 6.9 %collective-permute-start.8 = (bf16[4,2,1,32,256]{4,3,2,1,0:T(8,128)(2,1)S(1)}, bf16[4,2,1,32,256]{4,3,2,1,0:T(8,128)(2,1)S(1)}, u32[]{:S(2)}, u32[]{:S(2)}) collective-permute-start(bf16[4,2,1,32,256]{4,3,2,1,0:T(8,128)(2,1)S(1)} %get-tuple-element.44), channel_id=1, source_target_pairs={{0,124},{4,0},{8,4},{12,8},{16,12},{20,16},{24,20},{28,24},{32,28}... | collective-permute-start | bytes 393224 | tf_op jit(solution)/shard_map/ppermute | solution.py:492
  79.6 6.5 %collective-permute-start.9 = (bf16[4,2,1,32,256]{4,3,2,1,0:T(8,128)(2,1)S(1)}, bf16[4,2,1,32,256]{4,3,2,1,0:T(8,128)(2,1)S(1)}, u32[]{:S(2)}, u32[]{:S(2)}) collective-permute-start(bf16[4,2,1,32,256]{4,3,2,1,0:T(8,128)(2,1)S(1)} %get-tuple-element.46), channel_id=1, source_target_pairs={{0,4},{4,8},{8,12},{12,16},{16,20},{20,24},{24,28},{28,32},{32,36}... | collective-permute-start | bytes 393224 | tf_op jit(solution)/shard_map/ppermute | solution.py:492
  81.2 8.4 %collective-permute-start.10 = (bf16[4,2,1,32,256]{4,3,2,1,0:T(8,128)(2,1)S(1)}, bf16[4,2,1,32,256]{4,3,2,1,0:T(8,128)(2,1)S(1)}, u32[]{:S(2)}, u32[]{:S(2)}) collective-permute-start(bf16[4,2,1,32,256]{4,3,2,1,0:T(8,128)(2,1)S(1)} %get-tuple-element.47), channel_id=1, source_target_pairs={{0,8},{4,12},{8,16},{12,20},{16,24},{20,28},{24,32},{28,36},{32,40... | collective-permute-start | bytes 393224 | tf_op jit(solution)/shard_map/ppermute | solution.py:492
  89.5 5.6 %collective-permute-start.13 = (bf16[5,2,1,32,256]{4,3,2,1,0:T(8,128)(2,1)S(1)}, bf16[5,2,1,32,256]{4,3,2,1,0:T(8,128)(2,1)S(1)}, u32[]{:S(2)}, u32[]{:S(2)}) collective-permute-start(bf16[5,2,1,32,256]{4,3,2,1,0:T(8,128)(2,1)S(1)} %get-tuple-element.70), channel_id=1, source_target_pairs={{0,3},{1,0},{2,1},{3,2},{4,7},{5,4},{6,5},{7,6},{8,11},{9,8},{10,9... | collective-permute-start | bytes 491528 | tf_op jit(solution)/shard_map/ppermute | solution.py:492
  89.7 6.8 %collective-permute-start.12 = (bf16[5,2,1,32,256]{4,3,2,1,0:T(8,128)(2,1)S(1)}, bf16[5,2,1,32,256]{4,3,2,1,0:T(8,128)(2,1)S(1)}, u32[]{:S(2)}, u32[]{:S(2)}) collective-permute-start(bf16[5,2,1,32,256]{4,3,2,1,0:T(8,128)(2,1)S(1)} %get-tuple-element.71), channel_id=1, source_target_pairs={{0,2},{1,3},{2,0},{3,1},{4,6},{5,7},{6,4},{7,5},{8,10},{9,11},{10,... | collective-permute-start | bytes 491528 | tf_op jit(solution)/shard_map/ppermute | solution.py:492
  90.2 10.6 %collective-permute-start.11 = (bf16[5,2,1,32,256]{4,3,2,1,0:T(8,128)(2,1)S(1)}, bf16[5,2,1,32,256]{4,3,2,1,0:T(8,128)(2,1)S(1)}, u32[]{:S(2)}, u32[]{:S(2)}) collective-permute-start(bf16[5,2,1,32,256]{4,3,2,1,0:T(8,128)(2,1)S(1)} %get-tuple-element.72), channel_id=1, source_target_pairs={{0,1},{1,2},{2,3},{3,0},{4,5},{5,6},{6,7},{7,4},{8,9},{9,10},{10,1... | collective-permute-start | bytes 491528 | tf_op jit(solution)/shard_map/ppermute | solution.py:492
